TPU v7x, 32 devices: a whole 2x2x4 slice. The times are simulated.
32 devices in a mesh: seq: 8 (over y, x, core), head: 4 (over z).
Axes of the slice: x: 2, y: 2, z: 4, core: 2. Of those that a mesh axis runs over, the one named last changes fastest.
Arguments:
- mixer_input: bfloat16 [12288, 4096], P('seq', 'head'), may hold values from -6 to 6
- gate_input: bfloat16 [12288, 4096], P('seq', 'head'), may hold values from -6 to 6
- state_maps: bfloat16 [4, 12288, 128], P(None, 'seq'), may hold values from -0.375 to 0.375
- step_size: float32 [2, 64, 12288], P(None, 'head', 'seq'), may hold values from 0.2 to 2
- log_decay: float32 [2, 64, 12288], P(None, 'head', 'seq'), may hold values from -2 to 0
- skip_weight: float32 [64], P('head'), may hold values from 0.5 to 1.5
- doc_ids: int32 [12288], P('seq'), may hold values from 0 to 3, never falling along the last dimension, each value on 1 to 6144 neighbouring positions
- norm_gain: float32 [4096], P('head'), may hold values from 0.1 to 1.9
Outputs:
- mixed: bfloat16 [12288, 4096], P('seq', 'head')
Inputs may be any that keep to these rules, and one draw needn't show every extreme that they name: `doc_ids`: ids never fall along the sequence; each of the 4 documents holds 1 to 6144 tokens, one exactly 6144.
All inputs are finite; a program needn't handle non-finite values.
Results may differ from a plain program's by a relative error of at most 0.0054.
Values sent between devices are 32-bit elements; how exact they have to be, the bound alone decides.
A program may use at most 256 MiB of HBM per device.

v0:
```python
import jax
import jax.numpy as jnp
from jax import lax
from jax.sharding import PartitionSpec as P

BLOCK = 128


def prefix(part, axis, combine, identity, reverse):
    count = lax.axis_size(axis)
    place = lax.axis_index(axis)
    ahead = count - 1 - place if reverse else place
    gathered = jax.tree.map(lambda a: lax.all_gather(a, axis), part)
    state = jax.tree.map(lambda a, e: jnp.zeros_like(a) + jnp.asarray(e, a.dtype), part, identity)

    def one(step, state):
        source = count - 1 - step if reverse else step
        return combine(
            state, jax.tree.map(lambda a: lax.dynamic_index_in_dim(a, source, 0, False), gathered)
        )

    return lax.fori_loop(0, ahead, one, state)


def combine(earlier, later):
    decay_first, state_first, enter_first, leave_first = earlier
    decay_second, state_second, enter_second, leave_second = later
    keeping = ((leave_first == enter_second) | (enter_first < 0.0) | (enter_second < 0.0)).astype(
        jnp.float32
    )
    carried = decay_second * keeping
    return (
        carried * decay_first,
        state_second + carried[:, None, None] * state_first,
        jnp.where(enter_first < 0.0, enter_second, enter_first),
        jnp.where(leave_second < 0.0, leave_first, leave_second),
    )


def local_pass(blocks_x, b_rows, c_rows, decay_rows, step_rows, doc_rows):
    block_count = blocks_x.shape[0]
    head_count = decay_rows.shape[0]
    b_blocks = b_rows.reshape(block_count, BLOCK, -1)
    c_blocks = c_rows.reshape(block_count, BLOCK, -1)
    cumulative = jnp.cumsum(decay_rows.reshape(head_count, block_count, BLOCK), axis=2)
    step_blocks = step_rows.reshape(head_count, block_count, BLOCK)
    doc_blocks = doc_rows.reshape(block_count, BLOCK)
    scores = jnp.einsum("btn,bsn->bts", c_blocks, b_blocks, preferred_element_type=jnp.float32)
    places = jnp.arange(BLOCK)
    strict = (places[:, None] > places[None, :])[None] & (
        doc_blocks[:, :, None] == doc_blocks[:, None, :]
    )
    spread = jnp.where(strict[None], cumulative[:, :, :, None] - cumulative[:, :, None, :], 0.0)
    weights = jnp.where(
        strict[None], scores[None] * jnp.exp(spread) * step_blocks[:, :, None, :], 0.0
    )
    weights = weights.astype(jnp.bfloat16)
    inside_out = jnp.einsum(
        "hbts,bshp->bthp", weights, blocks_x, preferred_element_type=jnp.float32
    )
    last_ids = doc_blocks[:, -1]
    same_end = doc_blocks == last_ids[:, None]
    to_end = jnp.where(
        same_end[None], jnp.exp(cumulative[:, :, -1:] - cumulative) * step_blocks, 0.0
    )
    weighted_b = (b_blocks.astype(jnp.float32)[None] * to_end[..., None]).astype(jnp.bfloat16)
    local_states = jnp.einsum(
        "hbsn,bshp->bhnp", weighted_b, blocks_x, preferred_element_type=jnp.float32
    )
    prior_ids = jnp.concatenate([doc_rows[:1], last_ids[:-1]])
    block_decay = (
        jnp.exp(cumulative[:, :, -1]).T * (last_ids == prior_ids).astype(jnp.float32)[:, None]
    )

    def advance(carried_pair, block_item):
        state_now, factor_now = carried_pair
        local_now, decay_now = block_item
        return (
            (decay_now[:, None, None] * state_now + local_now, factor_now * decay_now),
            (state_now, factor_now),
        )

    start_state = jnp.zeros(local_states.shape[1:], jnp.float32)
    start_factor = jnp.ones((head_count,), jnp.float32)
    (final_state, total_decay), (starts, factors) = lax.scan(
        advance, (start_state, start_factor), (local_states, block_decay)
    )
    summary = (
        total_decay,
        final_state,
        doc_rows[:1].astype(jnp.float32),
        doc_rows[-1:].astype(jnp.float32),
    )
    return (inside_out, cumulative, starts, factors, prior_ids, summary)


def finish(c_rows, doc_rows, parts, incoming):
    inside_out, cumulative, starts, factors, prior_ids, summary = parts
    block_count = starts.shape[0]
    matching = (incoming[3] == doc_rows[:1].astype(jnp.float32)).astype(jnp.float32)
    arriving = incoming[1] * matching[:, None, None]
    entering = (starts + factors[:, :, None, None] * arriving[None]).astype(jnp.bfloat16)
    c_blocks = c_rows.reshape(block_count, BLOCK, -1)
    carried = jnp.einsum("btn,bhnp->bthp", c_blocks, entering, preferred_element_type=jnp.float32)
    doc_blocks = doc_rows.reshape(block_count, BLOCK)
    same_doc = (doc_blocks == prior_ids[:, None]).astype(jnp.float32)
    carry_reach = jnp.exp(cumulative).transpose(1, 2, 0) * same_doc[:, :, None]
    return inside_out + carried * carry_reach[..., None]


def local(
    mixer_input, gate_input, state_maps, step_size, log_decay, skip_weight, doc_ids, norm_gain
):
    tokens = mixer_input.shape[0]
    head_count = step_size.shape[1]
    head_width = mixer_input.shape[1] // head_count
    state_dim = state_maps.shape[2]
    block_count = tokens // BLOCK
    per_token = mixer_input.reshape(tokens, head_count, head_width)
    forward_x = per_token.reshape(block_count, BLOCK, head_count, head_width)
    backward_x = per_token[::-1].reshape(block_count, BLOCK, head_count, head_width)
    reversed_docs = doc_ids[::-1]
    reversed_c = state_maps[3][::-1]
    fwd_parts = local_pass(
        forward_x, state_maps[0], state_maps[1], log_decay[0], step_size[0], doc_ids
    )
    bwd_parts = local_pass(
        backward_x,
        state_maps[2][::-1],
        reversed_c,
        log_decay[1][:, ::-1],
        step_size[1][:, ::-1],
        reversed_docs,
    )
    fwd_sum = fwd_parts[5]
    bwd_sum = bwd_parts[5]
    neutral = (
        jnp.ones((head_count,), jnp.float32),
        jnp.zeros((head_count, state_dim, head_width), jnp.float32),
        -jnp.ones((1,), jnp.float32),
        -jnp.ones((1,), jnp.float32),
    )
    fwd_in = prefix(
        (fwd_sum[0], fwd_sum[1], fwd_sum[2], fwd_sum[3]), "seq", combine, neutral, False
    )
    bwd_in = prefix((bwd_sum[0], bwd_sum[1], bwd_sum[2], bwd_sum[3]), "seq", combine, neutral, True)
    forward_out = finish(state_maps[1], doc_ids, fwd_parts, fwd_in).reshape(
        tokens, head_count, head_width
    )
    backward_out = finish(reversed_c, reversed_docs, bwd_parts, bwd_in).reshape(
        tokens, head_count, head_width
    )[::-1]
    combined = (
        forward_out + backward_out + skip_weight[None, :, None] * per_token.astype(jnp.float32)
    )
    gate_wide = gate_input.astype(jnp.float32).reshape(tokens, head_count, head_width)
    gated_out = (combined * jax.nn.silu(gate_wide)).reshape(tokens, head_count * head_width)
    partial_squares = jnp.sum(gated_out * gated_out, axis=1)
    square_total = lax.psum(partial_squares, "head")
    channels = lax.axis_size("head") * head_count * head_width
    inverse_rms = lax.rsqrt(square_total / channels + 1e-05)
    return (gated_out * inverse_rms[:, None] * norm_gain[None, :]).astype(jnp.bfloat16)


def solution(mesh):
    return jax.shard_map(
        local,
        mesh=mesh,
        in_specs=(
            P("seq", "head"),
            P("seq", "head"),
            P(None, "seq", None),
            P(None, "head", "seq"),
            P(None, "head", "seq"),
            P("head"),
            P("seq"),
            P("head"),
        ),
        out_specs=P("seq", "head"),
        check_vma=False,
    )
```

profile of v0, /device:TPU:0, one launch (start us, length us, event | category | flops | bytes accessed | tf_op | source)
XLA Modules:
  0.0 315.6 jit_solution(17336573197923804926)
XLA Ops:
  9.6 1.5 slice_reduce_fusion.5
  13.0 2.4 fusion.58
  15.4 4.6 %copy.124 = bf16[1536,1024]{0,1:T(8,128)(2,1)} copy(bf16[1536,1024]{1,0:T(8,128)(2,1)} %param.16) | data formatting | bytes 6291456 | tf_op args[0]
  20.0 4.5 %reduce_window_sum.17 = f32[16,12,128]{2,1,0:T(8,128)S(1)} reduce-window(f32[16,12,128]{2,1,0:T(8,128)S(1)} %reshape_squeeze.13, f32[]{:T(128)} %constant.111.clone.1), window={size=1x1x128 pad=0_0x0_0x127_0}, to_apply=%region_0.0 | reduce-window | flops 3121152 | bytes 196612 | tf_op jit(solution)/shard_map/jit(cumsum)/reduce_window_sum | solution.py:45
  26.4 6.9 %reshape_reshape.3 = bf16[12,128,16,64]{1,0,3,2:T(8,128)(2,1)} reshape(bf16[1536,1024]{0,1:T(8,128)(2,1)} %copy.124) | data formatting | bytes 6291456 | tf_op jit(solution)/shard_map/reshape;reshape | solution.py:120
  34.1 10.4 %fusion.16 = f32[12,16,128,64]{3,2,1,0:T(8,128)} fusion(f32[16,12,128]{2,0,1:T(8,128)S(1)} %copy.126, f32[12,128,128]{2,1,0:T(8,128)S(1)} %convert_element_type.77, bf16[12,128,16,64]{1,0,3,2:T(8,128)(2,1)} %reshape_reshape.3), kind=kOutput, calls=%fused_computation.42 | convolution fusion | flops 408944640 | bytes 10321920 | tf_op jit(solution)/shard_map/hbsn,bshp->bhnp/dot_general | solution.py:67
  44.5 6.1 %broadcast.140.clone.1 = f32[12,16,128,64]{3,2,1,0:T(8,128)} broadcast(f32[]{:T(128)} %constant.111.clone.1), dimensions={} | broadcast | bytes 6291460 | tf_op jit(solution)/shard_map/broadcast.7
  50.6 30.8 %while.70 = (s32[]{:T(128)}, f32[16,128,64]{2,1,0:T(8,128)S(1)}, f32[16]{0:T(128)S(1)}, f32[12,16,128,64]{3,2,1,0:T(8,128)}, f32[12,16]{1,0:T(8,128)S(1)}, /*ind...) while((s32[]{:T(128)}, f32[16,128,64]{2,1,0:T(8,128)S(1)}, ...), condition=%wide.region_2.3_spmd.clone, body=%wide.region_1.2_spmd.clone.sunk | while | flops 524323 | bytes 3146869 | solution.py:85
  51.7 1.4 bitcast_add_fusion.11
  54.3 1.4 bitcast_add_fusion.11
  56.9 1.4 bitcast_add_fusion.11
  59.4 1.4 bitcast_add_fusion.11
  83.8 4.6 %reduce_window_sum.18 = f32[16,12,128]{2,1,0:T(8,128)S(1)} reduce-window(f32[16,12,128]{2,1,0:T(8,128)S(1)} %reshape.215, f32[]{:T(128)} %constant.111.clone.1), window={size=1x1x128 pad=0_0x0_0x127_0}, to_apply=%region_5.6 | reduce-window | flops 3121152 | bytes 196612 | tf_op jit(solution)/shard_map/jit(cumsum)/reduce_window_sum | solution.py:45
  92.1 8.8 %rev.26 = bf16[1536,16,64]{0,2,1:T(8,128)(2,1)} reverse(bf16[1536,16,64]{0,2,1:T(8,128)(2,1)} %bitcast.170), dimensions={0} | reverse | bytes 6291456 | tf_op jit(solution)/shard_map/rev | solution.py:121
  100.8 1.5 convert_reduce_fusion
  102.4 10.3 %fusion.18 = f32[12,16,128,64]{3,2,1,0:T(8,128)} fusion(f32[16,12,128]{2,0,1:T(8,128)} %copy.140, f32[12,128,128]{2,1,0:T(8,128)S(1)} %convert_element_type.84, bf16[1536,16,64]{0,2,1:T(8,128)(2,1)} %rev.26), kind=kOutput, calls=%fused_computation.44 | convolution fusion | flops 408944640 | bytes 10321920 | tf_op jit(solution)/shard_map/hbsn,bshp->bhnp/dot_general | solution.py:67
  112.7 6.1 %broadcast.140.clone = f32[12,16,128,64]{3,2,1,0:T(8,128)} broadcast(f32[]{:T(128)} %constant.111.clone.1), dimensions={} | broadcast | bytes 6291460 | tf_op jit(solution)/shard_map/broadcast.7
  118.8 30.9 %while.71 = (s32[]{:T(128)}, f32[16,128,64]{2,1,0:T(8,128)S(1)}, f32[16]{0:T(128)S(1)}, f32[12,16,128,64]{3,2,1,0:T(8,128)}, f32[12,16]{1,0:T(8,128)S(1)}, /*ind...) while((s32[]{:T(128)}, f32[16,128,64]{2,1,0:T(8,128)S(1)}, ...), condition=%wide.region_7.8_spmd.clone, body=%wide.region_6.7_spmd.clone.sunk | while | flops 524323 | bytes 3146869 | solution.py:85
  135.4 1.4 bitcast_add_fusion.12
  155.5 15.5 %all-reduce.4 = (f32[128]{0:T(128)S(1)}, f32[8]{0:T(128)S(1)}, f32[8]{0:T(128)S(1)}, f32[128]{0:T(128)S(1)}) all-reduce(f32[128]{0:T(128)S(1)} %dynamic-update-slice.3, f32[8]{0:T(128)S(1)} %convert_dynamic-update-slice_fusion, f32[8]{0:T(128)S(1)} %convert_dynamic-update-slice_fusion.1, ...), channel_id=7, replica_groups=mesh['seq'=8,'head'=4] {'seq'}, use_global_device_ids=true, to_apply=%add.3 | all-reduce | flops 272 | bytes 2176
  172.8 5.0 %copy.149 = bf16[1536,1024]{0,1:T(8,128)(2,1)} copy(bf16[1536,1024]{1,0:T(8,128)(2,1)} %param.17) | data formatting | bytes 6291456 | tf_op args[1]
  179.2 9.2 %fusion.10 = f32[12,16,128,64]{2,3,1,0:T(8,128)} fusion(f32[16,12,128]{2,0,1:T(8,128)S(1)} %copy.123, f32[16,12,128]{2,0,1:T(8,128)S(1)} %copy.121, f32[12,128,128]{2,1,0:T(8,128)S(1)} %fusion.63, pred[12,128,128]{2,1,0:T(8,128)(4,1)S(1)} %get-tuple-element.557, bf16[12,128,16,64]{1,0,3,2:T(8,128)(2,1)} %reshape_reshape.3), kind=kOutput, calls=%fused_computation.36 | convolution fusion | flops 421527552 | bytes 10616832 | tf_op jit(solution)/shard_map/hbts,bshp->bthp/dot_general | solution.py:58
  188.4 8.6 %fusion.11 = f32[12,16,128,64]{2,3,1,0:T(8,128)} fusion(f32[16,12,128]{2,0,1:T(8,128)S(1)} %copy_bitcast_fusion.1, f32[16,12,128]{2,0,1:T(8,128)S(1)} %copy.135, f32[12,128,128]{2,1,0:T(8,128)S(1)} %fusion.64, pred[12,128,128]{2,1,0:T(8,128)(4,1)S(1)} %get-tuple-element.558, bf16[1536,16,64]{0,2,1:T(8,128)(2,1)S(1)} %copy-done.3), kind=kOutput, calls=%fused_computation.37 | convolution fusion | flops 421527552 | bytes 10616832 | tf_op jit(solution)/shard_map/hbts,bshp->bthp/dot_general | solution.py:58
  198.2 40.0 %while.69 = (s32[]{:T(128)}, f32[16,128,64]{2,1,0:T(8,128)S(1)}, f32[1]{0:T(128)}, f32[1]{0:T(128)}, s32[]{:T(128)}, /*index=5*/f32[8,16,128,64]{2,3,1,0:T(8,128...) while((s32[]{:T(128)}, f32[16,128,64]{2,1,0:T(8,128)S(1)}, ...), condition=%wide.region_9.10_spmd, body=%wide.region_8.9_spmd.sunk | while | flops 262175 | bytes 3670492 | solution.py:22
  238.3 12.6 %fusion.24 = f32[12,16,8,8,128]{4,3,2,1,0:T(8,128)} fusion(f32[12,16,128,64]{2,3,1,0:T(8,128)} %fusion.11, f32[12,128,16]{1,2,0:T(8,128)S(1)} %copy-done.9, bf16[12,128,128,1]{2,1,3,0:T(8,128)(2,1)S(1)} %bitcast.179, f32[12,16,128,64]{3,2,1,0:T(8,128)} %get-tuple-element.305, f32[16,128,64]{2,1,0:T(8,128)S(1)} %broadcast_multiply_fusion, ...), kind=kOutput, calls=%fused_computation.54 | convolution fusion | flops 410517504 | bytes 19890944 | tf_op jit(solution)/shard_map/btn,bhnp->bthp/dot_general | solution.py:104
  251.0 6.2 %copy.179 = f32[12,16,8,8,128]{4,3,0,2,1:T(8,128)} copy(f32[12,16,8,8,128]{4,3,2,1,0:T(8,128)} %fusion.24) | data formatting | bytes 12582912 | tf_op jit(solution)/shard_map/reshape | solution.py:150
  257.2 10.5 %rev.27 = f32[1536,16,64]{0,2,1:T(8,128)} reverse(f32[1536,16,64]{0,2,1:T(8,128)} %bitcast.171), dimensions={0} | reverse | bytes 12582912 | tf_op jit(solution)/shard_map/rev | solution.py:150
  268.7 13.0 %fusion.26 = f32[12,16,8,8,128]{4,3,2,1,0:T(8,128)} fusion(f32[12,16,128,64]{2,3,1,0:T(8,128)} %fusion.10, f32[12,128,16]{1,2,0:T(8,128)} %copy.133, bf16[12,128,128,1]{2,1,3,0:T(8,128)(2,1)S(1)} %bitcast.177, f32[12,16,128,64]{3,2,1,0:T(8,128)} %get-tuple-element.299, f32[16,128,64]{2,1,0:T(8,128)} %broadcast_multiply_fusion.1, f32[12,16]{1,0:T(8,128)S(1)} %copy-done.11), kind=kOutput, calls=%fused_computation.57 | convolution fusion | flops 410517504 | bytes 19890944 | tf_op jit(solution)/shard_map/btn,bhnp->bthp/dot_general | solution.py:104
  281.8 8.6 %multiply_reduce_fusion = (f32[1536]{0:T(1024)S(1)}, f32[1536,16,64]{0,2,1:T(8,128)}) fusion(f32[16]{0:T(128)S(1)} %copy-done.16, f32[1536,16,64]{0,2,1:T(8,128)} %rev.27, f32[12,16,8,8,128]{4,3,2,1,0:T(8,128)} %fusion.26, bf16[1536,1024]{0,1:T(8,128)(2,1)} %copy.149, bf16[1536,1024]{0,1:T(8,128)(2,1)S(1)} %copy-done.2), kind=kLoop, calls=%fused_computation.58 | loop fusion | flops 18872832 | bytes 25172032 | tf_op jit(solution)/shard_map/reduce_sum | solution.py:158
  290.3 12.1 %psum.7 = f32[1536]{0:T(1024)S(1)} all-reduce(f32[1536]{0:T(1024)S(1)} %get-tuple-element.537), channel_id=1, replica_groups=mesh['seq'=8,'head'=4] {'head'}, use_global_device_ids=true, to_apply=%region_11.12 | all-reduce | flops 1536 | bytes 12288 | tf_op jit(solution)/shard_map/psum | solution.py:159
  302.5 3.4 %fusion.22 = bf16[1536,1024]{0,1:T(8,128)(2,1)S(1)} fusion(f32[1536,16,64]{0,2,1:T(8,128)} %get-tuple-element.538, f32[1024]{0:T(1024)S(1)} %copy-done.15, f32[1536]{0:T(1024)S(1)} %add_rsqrt_fusion), kind=kLoop, calls=%fused_computation.51 | loop fusion | flops 4718592 | bytes 9447424 | tf_op jit(solution)/shard_map/convert_element_type | solution.py:162
  305.9 2.9 copy.150
  (234 shorter events, 93.4 us)
Async XLA Ops:
  6.5 18.9 %copy-start.8 = (s32[1536]{0:T(1024)S(1)}, s32[1536]{0:T(1024)}, u32[]{:S(2)}) copy-start(s32[1536]{0:T(1024)} %param.22) | copy-start | bytes 18436
  6.5 190.5 %all-gather.9.cloned.1.call-start = ((), (), s32[]{:S(2)}) async-start(), calls=%async_computation | async-start | bytes 4718592 | tf_op jit(solution)/shard_map/all_gather | solution.py:13
  50.6 41.0 %copy-start.5 = (bf16[1536,128]{1,0:T(8,128)(2,1)S(1)}, bf16[1536,128]{1,0:T(8,128)(2,1)}, u32[]{:S(2)}) copy-start(bf16[1536,128]{1,0:T(8,128)(2,1)} %get-tuple-element.547) | copy-start | bytes 1179652
  81.4 1.4 copy-start.12
  81.4 10.2 %copy-start.10 = (f32[12,16]{1,0:T(8,128)}, f32[12,16]{1,0:T(8,128)S(1)}, u32[]{:S(2)}) copy-start(f32[12,16]{1,0:T(8,128)S(1)} %get-tuple-element.300) | copy-start | bytes 2308
  82.6 114.6 %all-gather.11.cloned.1.call-start = ((), (), s32[]{:S(2)}) async-start(), calls=%async_computation.1 | async-start | bytes 4718592 | tf_op jit(solution)/shard_map/all_gather | solution.py:13
  112.7 6.1 %copy-start.14 = (f32[16]{0:T(128)S(1)}, f32[16]{0:T(128)}, u32[]{:S(2)}) copy-start(f32[16]{0:T(128)} %custom-call.3) | copy-start | bytes 196
  118.8 33.5 %copy-start.17 = (u32[32]{0:T(128)S(1)}, u32[32]{0:T(128)}, u32[]{:S(2)}) copy-start(u32[32]{0:T(128)} %constant.122) | copy-start | bytes 388
  118.8 34.9 %copy-start.13 = (f32[16]{0:T(128)S(1)}, f32[16]{0:T(128)}, u32[]{:S(2)}) copy-start(f32[16]{0:T(128)} %copy-done.12) | copy-start | bytes 196
  118.8 52.2 %copy-start.6 = (f32[12,128,16]{1,0,2:T(8,128)S(1)}, f32[12,128,16]{1,0,2:T(8,128)}, u32[]{:S(2)}) copy-start(f32[12,128,16]{1,0,2:T(8,128)} %get-tuple-element.553) | copy-start | bytes 294916
  118.8 53.0 %copy-start.7 = (f32[12,128,16]{1,0,2:T(8,128)S(1)}, f32[12,128,16]{1,0,2:T(8,128)}, u32[]{:S(2)}) copy-start(f32[12,128,16]{1,0,2:T(8,128)} %get-tuple-element.556) | copy-start | bytes 294916
  118.8 53.6 %copy-start.4 = (bf16[1536,128]{1,0:T(8,128)(2,1)S(1)}, bf16[1536,128]{1,0:T(8,128)(2,1)}, u32[]{:S(2)}) copy-start(bf16[1536,128]{1,0:T(8,128)(2,1)} %get-tuple-element.548) | copy-start | bytes 1179652
  179.2 9.2 %copy-start.3 = (bf16[1536,16,64]{0,2,1:T(8,128)(2,1)S(1)}, bf16[1536,16,64]{0,2,1:T(8,128)(2,1)}, u32[]{:S(2)}) copy-start(bf16[1536,16,64]{0,2,1:T(8,128)(2,1)} %rev.26) | copy-start | bytes 9437188
  197.1 0.9 copy-start
  198.2 40.1 %copy-start.9 = (f32[12,128,16]{1,2,0:T(8,128)S(1)}, f32[12,128,16]{1,2,0:T(8,128)}, u32[]{:S(2)}) copy-start(f32[12,128,16]{1,2,0:T(8,128)} %copy.147) | copy-start | bytes 294916
  257.2 10.5 %copy-start.1 = (f32[16,128,64]{2,1,0:T(8,128)S(1)}, f32[16,128,64]{2,1,0:T(8,128)}, u32[]{:S(2)}) copy-start(f32[16,128,64]{2,1,0:T(8,128)} %copy-done) | copy-start | bytes 1572868
  257.2 11.6 %copy-start.11 = (f32[12,16]{1,0:T(8,128)S(1)}, f32[12,16]{1,0:T(8,128)}, u32[]{:S(2)}) copy-start(f32[12,16]{1,0:T(8,128)} %copy-done.10) | copy-start | bytes 2308
  268.7 13.0 %copy-start.2 = (bf16[1536,1024]{0,1:T(8,128)(2,1)S(1)}, bf16[1536,1024]{0,1:T(8,128)(2,1)}, u32[]{:S(2)}) copy-start(bf16[1536,1024]{0,1:T(8,128)(2,1)} %copy.124) | copy-start | bytes 9437188
  268.7 13.0 %copy-start.16 = (f32[16]{0:T(128)S(1)}, f32[16]{0:T(128)}, u32[]{:S(2)}) copy-start(f32[16]{0:T(128)} %param.21) | copy-start | bytes 196
  281.8 20.7 %copy-start.15 = (f32[1024]{0:T(1024)S(1)}, f32[1024]{0:T(1024)}, u32[]{:S(2)}) copy-start(f32[1024]{0:T(1024)} %param.23) | copy-start | bytes 12292
Sparse Core Ops, SparseCore 0:
  82.7 39.4 all-gather.8
  151.1 39.5 all-gather.10
where the time goes:
time: 319 us; the launch traced here: 316 us
  local copies, waits for them, and re-layouts  91.5 us (29%)
  other arithmetic  91.5 us (29%)
  matrix products  65 us (20%)
  blocking collectives  27.6 us (9%)
  loops' own time  24.3 us (8%)
  between operations  15.6 us (5%)
    add x24, other arithmetic, advance(): decay_now[:, None, None] * state_now + local_now  34 us
    dynamic_update_slice x24, other arithmetic, local_pass(): lax.scan(advance, (start_state, start_factor), (local_states, block_decay))  25.9 us
    dot_general x2, matrix products, finish(): jnp.einsum('btn,bhnp->bthp', c_blocks, entering, preferred_element_type=j...  25.7 us
    another operation x2, loops' own time, prefix(): return lax.fori_loop(0, ahead, one, state)  23.8 us
    dot_general x2, matrix products, local_pass(): jnp.einsum('hbsn,bshp->bhnp', weighted_b, blocks_x, preferred_element_typ...  20.7 us
    dot_general x2, matrix products, local_pass(): jnp.einsum('hbts,bshp->bthp', weights, blocks_x, preferred_element_type=j...  17.8 us
    unnamed x1, blocking collectives  15.5 us
    dynamic_slice x21, local copies, waits for them, and re-layouts, one(): lax.dynamic_index_in_dim(a, source, 0, False)  14.6 us
  transfers between devices with their start and end apart: 2, of which 0 were waited for; matrix products, arithmetic and copies ran while one was open for 31% of the time, Pallas kernels for 0%

commit v1 on v0

v1 whole, which is shorter than its diff:
```python
import functools

import jax
import jax.numpy as jnp
from jax import lax
from jax.experimental import pallas as pl
from jax.experimental.pallas import tpu as pltpu
from jax.sharding import PartitionSpec as P

BLOCK = 128
ROWS = 136
F32 = jnp.float32
BF16 = jnp.bfloat16
HIGH = lax.Precision.HIGHEST


def iota(shape, axis):
    return lax.broadcasted_iota(jnp.int32, shape, axis)


def spread(columns, first, heads):
    rows = columns.shape[0]
    half = iota((rows, 128), 1) // 64
    parts = []
    for pair in range(heads // 2):
        index = first + 2 * pair + half
        parts.append(jnp.take_along_axis(columns, index, axis=1, mode="promise_in_bounds"))
    return jnp.concatenate(parts, axis=1)


def kernel(
    sizes, x_ref, gate_ref, maps_ref, step_ref, decay_ref, skip_ref, docs_ref, gain_ref, out_ref,
    own, other, total, slots, into, local, columns, rows, reach, state, state16, acc, squares, inverse,
    send_a, recv_a, send_b, recv_b, send_c, recv_c, send_h, recv_h,
):
    seq, head_ways, heads = sizes
    chips = seq // 2
    width = heads * 64
    half = width // 2
    blocks = x_ref.shape[0] // BLOCK
    place = lax.axis_index("seq")
    core = lax.rem(place, 2)
    chip = lax.div(place, 2)
    head_place = lax.axis_index("head")
    sibling = place + 1 - 2 * core

    def chip_at(offset):
        return {"seq": 2 * lax.rem(chip + offset, chips) + core}

    def head_at(offset):
        return {"head": lax.rem(head_place + offset, head_ways)}

    barrier = pltpu.get_barrier_semaphore()
    partners = [{"seq": sibling}]
    partners += [chip_at(o) for o in range(1, chips)] + [head_at(o) for o in range(1, head_ways)]
    for partner in partners:
        pl.semaphore_signal(barrier, inc=1, device_id=partner, device_id_type=pl.DeviceIdType.MESH)
    pl.semaphore_wait(barrier, len(partners))

    def remote(src, dst, send, recv, device):
        return pltpu.make_async_remote_copy(
            src_ref=src, dst_ref=dst, send_sem=send, recv_sem=recv,
            device_id=device, device_id_type=pl.DeviceIdType.MESH,
        )

    below = (iota((BLOCK, BLOCK), 0) <= iota((BLOCK, BLOCK), 1)).astype(F32)
    above = (iota((BLOCK, BLOCK), 0) >= iota((BLOCK, BLOCK), 1)).astype(F32)
    tile = iota((8, half), 0)

    def at(k):
        return pl.ds(pl.multiple_of(k * BLOCK, BLOCK), BLOCK)

    state[...] = jnp.zeros_like(state)
    first_doc = docs_ref[0:1, 0:1]
    last_doc = docs_ref[blocks - 1 : blocks, BLOCK - 1 : BLOCK]

    def summarize(k, carry):
        log_f, log_b, prior = carry
        docs = docs_ref[pl.ds(k, 1), :]
        first, last = docs[:, :1], docs[:, BLOCK - 1 :]
        cum_f = jnp.dot(decay_ref[0, :, at(k)], below, precision=HIGH, preferred_element_type=F32)
        cum_b = jnp.dot(decay_ref[1, :, at(k)], above, precision=HIGH, preferred_element_type=F32)
        step_f, step_b = step_ref[0, :, at(k)], step_ref[1, :, at(k)]
        in_f = jnp.where(docs == last, jnp.exp(cum_f[:, BLOCK - 1 :] - cum_f) * step_f, 0.0)
        in_b = jnp.where(docs == first, jnp.exp(cum_b[:, :1] - cum_b) * step_b, 0.0)
        pad = jnp.zeros((BLOCK - 4 * heads, BLOCK), F32)
        cols = jnp.concatenate([cum_f, cum_b, in_f, in_b, pad], axis=0).T
        columns[at(k), :] = cols
        rows[k, 0] = cum_f - jnp.log(step_f)
        rows[k, 1] = cum_b - jnp.log(step_b)
        reach[k, 0] = cum_f
        reach[k, 1] = cum_b
        x = x_ref[at(k), :].astype(F32)
        put_f = (x * spread(cols, 2 * heads, heads)).astype(BF16)
        put_b = (x * spread(cols, 3 * heads, heads)).astype(BF16)
        map_f = maps_ref[0, at(k), :].astype(F32).T.astype(BF16)
        map_b = maps_ref[2, at(k), :].astype(F32).T.astype(BF16)
        local_f = jnp.dot(map_f, put_f, preferred_element_type=F32)
        local_b = jnp.dot(map_b, put_b, preferred_element_type=F32)
        local[0, k] = local_f
        local[1, k] = local_b
        block_f = spread(cols[BLOCK - 8 :], 0, heads)[7:]
        block_b = spread(cols[:8], heads, heads)[:1]
        keep = jnp.exp(block_f) * (prior == last).astype(F32)
        state[0] = state[0] * keep + local_f
        state[1] = state[1] + local_b * (jnp.exp(log_b) * (first == first_doc).astype(F32))
        return log_f + block_f, log_b + block_b, last

    zero = jnp.zeros((1, width), F32)
    logs = lax.fori_loop(0, blocks, summarize, (zero, zero, jnp.full((1, 1), -1.0, F32)))
    for g in range(2):
        part = slice(g * half, (g + 1) * half)
        for d, doc in ((0, last_doc), (1, first_doc)):
            own[g, d, 0:128, :] = state[d, :, part]
            own[g, d, 128:ROWS, :] = jnp.where(tile == 0, logs[d][:, part], doc)

    to_sibling = remote(own, other, send_a, recv_a, {"seq": sibling})
    to_sibling.start()

    low = iota((BLOCK, BLOCK), 1) < iota((BLOCK, BLOCK), 0)
    diagonal = iota((BLOCK, BLOCK), 1) == iota((BLOCK, BLOCK), 0)
    left = iota((BLOCK, BLOCK), 1) < 64

    def inside(k, carry):
        docs = jnp.broadcast_to(docs_ref[pl.ds(k, 1), :], (BLOCK, BLOCK))
        dims = (((1,), (1,)), ((), ()))
        score_f = lax.dot_general(maps_ref[1, at(k), :], maps_ref[0, at(k), :], dims, preferred_element_type=F32)
        score_b = lax.dot_general(maps_ref[3, at(k), :], maps_ref[2, at(k), :], dims, preferred_element_type=F32)
        same = (docs == docs.T) & jnp.logical_not(diagonal)
        score = jnp.where(same, jnp.where(low, score_f, score_b), 0.0)
        cols = columns[at(k), :]
        row_f, row_b = rows[k, 0], rows[k, 1]
        for pair in range(heads // 2):
            lanes = slice(pair * 128, pair * 128 + 128)
            x = x_ref[at(k), lanes]
            weights = []
            for h in (2 * pair, 2 * pair + 1):
                power = jnp.where(
                    low,
                    cols[:, h : h + 1] - row_f[h : h + 1],
                    cols[:, heads + h : heads + h + 1] - row_b[h : h + 1],
                )
                weights.append((score * jnp.exp(power)).astype(BF16))
            none = jnp.zeros_like(x)
            values = jnp.concatenate([jnp.where(left, x, none), jnp.where(left, none, x)], axis=0)
            acc[at(k), lanes] = jnp.dot(
                jnp.concatenate(weights, axis=1), values, preferred_element_type=F32
            )
        return carry

    cut_a, cut_b = blocks // 4, blocks - blocks // 6
    lax.fori_loop(0, cut_a, inside, 0)
    to_sibling.wait()

    def join(later, earlier):
        log, doc = later[128:129], later[129:130]
        keep = jnp.exp(log) * (doc == earlier[129:130]).astype(F32)
        top = later[0:128] + keep * earlier[0:128]
        return top, jnp.where(tile == 0, log + earlier[128:129], doc)

    @pl.when(core == 0)
    def _():
        for d, (later, earlier) in ((0, (other, own)), (1, (own, other))):
            top, end = join(later[0, d], earlier[0, d])
            total[d, 0:128, :] = top
            total[d, 128:ROWS, :] = end

    @pl.when(core == 1)
    def _():
        for d, (later, earlier) in ((0, (own, other)), (1, (other, own))):
            top, end = join(later[1, d], earlier[1, d])
            total[d, 0:128, :] = top
            total[d, 128:ROWS, :] = end

    to_chips = []
    for o in range(1, chips):
        way = jnp.where(chip + o < chips, 0, 1)
        to_chips.append(remote(total.at[way], slots.at[o], send_b.at[o], recv_b.at[o], chip_at(o)))
        to_chips[-1].start()
    lax.fori_loop(cut_a, cut_b, inside, 0)
    for copy in to_chips:
        copy.wait()

    for d in range(2):
        into[core, d, 0:128, :] = jnp.zeros((128, half), F32)
        into[core, d, 128:ROWS, :] = jnp.where(tile == 0, 0.0, -1.0)
        for o in range(1, chips):
            slot = o if d == 0 else chips - o
            there = chip >= o if d == 0 else chip + o < chips

            @pl.when(there)
            def _(d=d, o=o, slot=slot):
                part = slots[slot]
                log, doc = part[128:129], part[129:130]
                if o == 1:
                    into[core, d] = part
                else:
                    so_far = into[core, d, 128:ROWS, :]
                    keep = jnp.exp(so_far[0:1]) * (doc == so_far[1:2]).astype(F32)
                    into[core, d, 0:128, :] += keep * part[0:128]
                    into[core, d, 128:ROWS, :] = jnp.where(tile == 0, so_far[0:1] + log, so_far[1:2])

    share = remote(into.at[core], into.at[core], send_c, recv_c, {"seq": sibling})
    share.start()
    lax.fori_loop(cut_b, blocks, inside, 0)
    share.wait_send()
    remote(into.at[core], into.at[1 - core], send_c, recv_c, {"seq": sibling}).wait_recv()

    for d in range(2):
        for g in range(2):
            part = slice(g * half, (g + 1) * half)

            @pl.when(core == d)
            def _(d=d, g=g, part=part):
                state[d, :, part] = into[g, d, 0:128, :]
                if g == 0:
                    state16[d] = into[g, d, 128:ROWS, 0:128]

            @pl.when(core != d)
            def _(d=d, g=g, part=part):
                top, end = join(other[g, d], into[g, d])
                state[d, :, part] = top
                if g == 0:
                    state16[d] = end[:, 0:128]

    def leave(d, k, prior):
        docs = docs_ref[pl.ds(k, 1), :]
        cum = reach[k, d]
        carry = jnp.where(docs == prior, jnp.exp(cum), 0.0)
        cols = jnp.concatenate([carry, cum, jnp.zeros((BLOCK - 2 * heads, BLOCK), F32)], axis=0).T
        before = state[d]
        given = jnp.dot(maps_ref[2 * d + 1, at(k), :], before.astype(BF16), preferred_element_type=F32)
        if d == 0:
            block, last = spread(cols[BLOCK - 8 :], heads, heads)[7:], docs[:, BLOCK - 1 :]
        else:
            block, last = spread(cols[:8], heads, heads)[:1], docs[:, :1]
        state[d] = before * (jnp.exp(block) * (last == prior).astype(F32)) + local[d, k]
        return given * spread(cols, 0, heads), last

    def forward(k, prior):
        part, last = leave(0, k, prior)
        acc[at(k), :] += part
        return last

    lax.fori_loop(0, blocks, forward, state16[0, 1:2, 0:1])
    squares[0] = jnp.zeros((BLOCK, 128), F32)
    lane = iota((BLOCK, 128), 1)

    def backward(step, prior):
        k = blocks - 1 - step
        part, last = leave(1, k, prior)
        gate = gate_ref[at(k), :].astype(F32)
        mixed = acc[at(k), :] + part + skip_ref[...] * x_ref[at(k), :].astype(F32)
        gated = mixed * (gate / (1.0 + jnp.exp(-gate)))
        acc[at(k), :] = gated
        squares[0] += jnp.where(lane == k, jnp.sum(gated * gated, axis=1, keepdims=True), 0.0)
        return last

    lax.fori_loop(0, blocks, backward, state16[1, 1:2, 0:1])
    to_heads = [
        remote(squares.at[0], squares.at[o], send_h.at[o], recv_h.at[o], head_at(o))
        for o in range(1, head_ways)
    ]
    for copy in to_heads:
        copy.start()
    for copy in to_heads:
        copy.wait()
    sum_all = squares[0]
    for o in range(1, head_ways):
        sum_all = sum_all + squares[o]
    inverse[...] = lax.rsqrt(sum_all / (head_ways * width) + 1e-05)

    def scale(k, carry):
        factor = jnp.sum(jnp.where(lane == k, inverse[...], 0.0), axis=1, keepdims=True)
        out_ref[at(k), :] = (acc[at(k), :] * factor * gain_ref[...]).astype(BF16)
        return carry

    lax.fori_loop(0, blocks, scale, 0)


def local(
    mixer_input, gate_input, state_maps, step_size, log_decay, skip_weight, doc_ids, norm_gain
):
    tokens, width = mixer_input.shape
    heads = step_size.shape[1]
    blocks = tokens // BLOCK
    half = width // 2
    seq, head_ways = lax.axis_size("seq"), lax.axis_size("head")
    chips = seq // 2
    docs = doc_ids.reshape(blocks, BLOCK).astype(F32)
    skip = jnp.repeat(skip_weight, width // heads)[None, :]
    vmem = pl.BlockSpec(memory_space=pltpu.VMEM)
    return pl.pallas_call(
        functools.partial(kernel, (seq, head_ways, heads)),
        out_shape=jax.ShapeDtypeStruct((tokens, width), BF16),
        in_specs=[vmem] * 8,
        out_specs=vmem,
        scratch_shapes=[
            pltpu.VMEM((2, 2, ROWS, half), F32),
            pltpu.VMEM((2, 2, ROWS, half), F32),
            pltpu.VMEM((2, ROWS, half), F32),
            pltpu.VMEM((chips, ROWS, half), F32),
            pltpu.VMEM((2, 2, ROWS, half), F32),
            pltpu.VMEM((2, blocks, 128, width), F32),
            pltpu.VMEM((tokens, 128), F32),
            pltpu.VMEM((blocks, 2, heads, 128), F32),
            pltpu.VMEM((blocks, 2, heads, 128), F32),
            pltpu.VMEM((2, 128, width), F32),
            pltpu.VMEM((2, 8, 128), F32),
            pltpu.VMEM((tokens, width), F32),
            pltpu.VMEM((head_ways, BLOCK, 128), F32),
            pltpu.VMEM((BLOCK, 128), F32),
            pltpu.SemaphoreType.DMA,
            pltpu.SemaphoreType.DMA,
            pltpu.SemaphoreType.DMA((chips,)),
            pltpu.SemaphoreType.DMA((chips,)),
            pltpu.SemaphoreType.DMA,
            pltpu.SemaphoreType.DMA,
            pltpu.SemaphoreType.DMA((head_ways,)),
            pltpu.SemaphoreType.DMA((head_ways,)),
        ],
        compiler_params=pltpu.CompilerParams(
            collective_id=0, has_side_effects=True, vmem_limit_bytes=56 * 2**20
        ),
    )(mixer_input, gate_input, state_maps, step_size, log_decay, skip, docs, norm_gain[None, :])


def solution(mesh):
    return jax.shard_map(
        local,
        mesh=mesh,
        in_specs=(
            P("seq", "head"),
            P("seq", "head"),
            P(None, "seq", None),
            P(None, "head", "seq"),
            P(None, "head", "seq"),
            P("head"),
            P("seq"),
            P("head"),
        ),
        out_specs=P("seq", "head"),
        check_vma=False,
    )
```

time: 319 us -> 74.2 us (0.23); the launches traced: 316 us -> 74 us
  other arithmetic: 91.5 us -> 1.3 us
  local copies, waits for them, and re-layouts: 91.5 us -> 5.26 us
  Pallas kernels: 0 us -> 67.4 us
  matrix products: 65 us -> 0 us
  blocking collectives: 27.6 us -> 0 us
  loops' own time: 24.3 us -> 0 us
  between operations: 15.6 us -> 0.01 us
    pallas_call x0 -> x1, Pallas kernels: none -> 67.4 us  [local(): pl.pallas_call(functools.partial(kernel, (seq, head_ways, heads)), out_sh...]
    dot_general x8 -> x0, matrix products: 65 us -> none  [the longest x2 25.7 us: finish(): jnp.einsum('btn,bhnp->bthp', c_blocks, entering, preferred_element_type=j...]
    add x31 -> x0, other arithmetic: 35.5 us -> none  [the longest x24 34 us: advance(): decay_now[:, None, None] * state_now + local_now]
    dynamic_update_slice x24 -> x0, other arithmetic: 25.9 us -> none  [local_pass(): lax.scan(advance, (start_state, start_factor), (local_states, block_decay))]
    another operation x4 -> x0, loops' own time: 24.3 us -> none  [the longest x2 23.8 us: prefix(): return lax.fori_loop(0, ahead, one, state)]
    rev x7 -> x0, local copies, waits for them, and re-layouts: 22.6 us -> none  [the longest x1 10.5 us: local(): finish(reversed_c, reversed_docs, bwd_parts, bwd_in)]
    another operation x10 -> x1, local copies, waits for them, and re-layouts: 19.3 us -> 0.67 us  [local(): skip = jnp.repeat(skip_weight, width // heads)[None, :]]
    unnamed x1 -> x0, blocking collectives: 15.5 us -> none
  transfers between devices with their start and end apart: 2 -> 0, of which waited for: 0 -> 0; matrix products, arithmetic and copies ran while one was open for 31% -> 0% of each run, Pallas kernels for 0% -> 0%
where the time goes in v1:
time: 74.2 us; the launch traced here: 74 us
  Pallas kernels  67.4 us (91%)
  local copies, waits for them, and re-layouts  5.26 us (7%)
  other arithmetic  1.3 us (2%)
    pallas_call x1, Pallas kernels, local(): pl.pallas_call(functools.partial(kernel, (seq, head_ways, heads)), out_sh...  67.4 us
    unnamed x1, local copies, waits for them, and re-layouts  3.86 us

profile of v1, /device:TPU:0, one launch (start us, length us, event | category | flops | bytes accessed | tf_op | source)
XLA Modules:
  0.0 74.0 jit_solution(7356661683811768497)
XLA Ops:
  0.0 0.7 broadcast_in_dim.6
  0.7 0.7 broadcast_in_dim_reshape.3.skip_ref
  1.4 1.3 %convert_bitcast_fusion.docs_ref = f32[12,128]{1,0:T(8,128)} fusion(s32[1536]{0:T(1024)} %param.14), kind=kLoop, calls=%fused_computation | loop fusion | flops 1536 | bytes 12288 | tf_op jit(solution)/shard_map/convert_element_type | solution.py:290
  2.7 67.4 %shard_map.82 = bf16[1536,1024]{1,0:T(8,128)(2,1)} custom-call(bf16[1536,1024]{1,0:T(8,128)(2,1)} %x_ref.1, bf16[1536,1024]{1,0:T(8,128)(2,1)} %gate_ref.1, bf16[4,1536,128]{2,1,0:T(8,128)(2,1)} %maps_ref.1, f32[2,16,1536]{2,1,0:T(8,128)} %step_ref.1, f32[2,16,1536]{2,1,0:T(8,128)} %decay_ref.1, f32[1,1024]{1,0:T(1,128)} %broadcast_in_dim_reshape.3.skip_ref, ...), custom_call_target="tpu_custom_call" | custom-call | tf_op jit(solution)/shard_map/pallas_call | solution.py:293
  70.1 3.9 %copy.10 = bf16[1536,1024]{1,0:T(8,128)(2,1)} copy(bf16[1536,1024]{1,0:T(8,128)(2,1)} %shard_map.82) | data formatting | bytes 6291456

commit v2 on v1

--- a/solution.py
+++ b/solution.py
@@ -30,7 +30,7 @@
 
 def kernel(
     sizes, x_ref, gate_ref, maps_ref, step_ref, decay_ref, skip_ref, docs_ref, gain_ref, out_ref,
-    own, other, total, slots, into, local, columns, rows, reach, state, state16, acc, squares, inverse,
+    own, other, total, slots, into, local, columns, rows, gains, state, acc, squares, inverse,
     send_a, recv_a, send_b, recv_b, send_c, recv_c, send_h, recv_h,
 ):
     seq, head_ways, heads = sizes
@@ -71,25 +71,27 @@
         return pl.ds(pl.multiple_of(k * BLOCK, BLOCK), BLOCK)
 
     state[...] = jnp.zeros_like(state)
-    first_doc = docs_ref[0:1, 0:1]
-    last_doc = docs_ref[blocks - 1 : blocks, BLOCK - 1 : BLOCK]
+    first_doc = docs_ref[0:1, :].astype(F32)[:, :1]
+    last_doc = docs_ref[blocks - 1 : blocks, :].astype(F32)[:, BLOCK - 1 :]
 
     def summarize(k, carry):
         log_f, log_b, prior = carry
-        docs = docs_ref[pl.ds(k, 1), :]
+        docs = docs_ref[pl.ds(k, 1), :].astype(F32)
+        after = docs_ref[pl.ds(jnp.minimum(k + 1, blocks - 1), 1), :].astype(F32)
         first, last = docs[:, :1], docs[:, BLOCK - 1 :]
+        after = jnp.where(k == blocks - 1, last, after[:, :1])
         cum_f = jnp.dot(decay_ref[0, :, at(k)], below, precision=HIGH, preferred_element_type=F32)
         cum_b = jnp.dot(decay_ref[1, :, at(k)], above, precision=HIGH, preferred_element_type=F32)
         step_f, step_b = step_ref[0, :, at(k)], step_ref[1, :, at(k)]
         in_f = jnp.where(docs == last, jnp.exp(cum_f[:, BLOCK - 1 :] - cum_f) * step_f, 0.0)
         in_b = jnp.where(docs == first, jnp.exp(cum_b[:, :1] - cum_b) * step_b, 0.0)
-        pad = jnp.zeros((BLOCK - 4 * heads, BLOCK), F32)
-        cols = jnp.concatenate([cum_f, cum_b, in_f, in_b, pad], axis=0).T
+        out_f = jnp.where(docs == prior, jnp.exp(cum_f), 0.0)
+        out_b = jnp.where(docs == after, jnp.exp(cum_b), 0.0)
+        pad = jnp.zeros((BLOCK - 6 * heads, BLOCK), F32)
+        cols = jnp.concatenate([cum_f, cum_b, in_f, in_b, out_f, out_b, pad], axis=0).T
         columns[at(k), :] = cols
         rows[k, 0] = cum_f - jnp.log(step_f)
         rows[k, 1] = cum_b - jnp.log(step_b)
-        reach[k, 0] = cum_f
-        reach[k, 1] = cum_b
         x = x_ref[at(k), :].astype(F32)
         put_f = (x * spread(cols, 2 * heads, heads)).astype(BF16)
         put_b = (x * spread(cols, 3 * heads, heads)).astype(BF16)
@@ -102,12 +104,14 @@
         block_f = spread(cols[BLOCK - 8 :], 0, heads)[7:]
         block_b = spread(cols[:8], heads, heads)[:1]
         keep = jnp.exp(block_f) * (prior == last).astype(F32)
+        gains[k, 0:1, :] = keep
+        gains[k, 1:2, :] = jnp.exp(block_b) * (after == first).astype(F32)
         state[0] = state[0] * keep + local_f
         state[1] = state[1] + local_b * (jnp.exp(log_b) * (first == first_doc).astype(F32))
         return log_f + block_f, log_b + block_b, last
 
     zero = jnp.zeros((1, width), F32)
-    logs = lax.fori_loop(0, blocks, summarize, (zero, zero, jnp.full((1, 1), -1.0, F32)))
+    logs = lax.fori_loop(0, blocks, summarize, (zero, zero, first_doc))
     for g in range(2):
         part = slice(g * half, (g + 1) * half)
         for d, doc in ((0, last_doc), (1, first_doc)):
@@ -122,7 +126,7 @@
     left = iota((BLOCK, BLOCK), 1) < 64
 
     def inside(k, carry):
-        docs = jnp.broadcast_to(docs_ref[pl.ds(k, 1), :], (BLOCK, BLOCK))
+        docs = jnp.broadcast_to(docs_ref[pl.ds(k, 1), :].astype(F32), (BLOCK, BLOCK))
         dims = (((1,), (1,)), ((), ()))
         score_f = lax.dot_general(maps_ref[1, at(k), :], maps_ref[0, at(k), :], dims, preferred_element_type=F32)
         score_b = lax.dot_general(maps_ref[3, at(k), :], maps_ref[2, at(k), :], dims, preferred_element_type=F32)
@@ -206,57 +210,49 @@
     share.wait_send()
     remote(into.at[core], into.at[1 - core], send_c, recv_c, {"seq": sibling}).wait_recv()
 
-    for d in range(2):
+    for d, edge in ((0, first_doc), (1, last_doc)):
         for g in range(2):
             part = slice(g * half, (g + 1) * half)
 
             @pl.when(core == d)
-            def _(d=d, g=g, part=part):
-                state[d, :, part] = into[g, d, 0:128, :]
-                if g == 0:
-                    state16[d] = into[g, d, 128:ROWS, 0:128]
+            def _(d=d, g=g, part=part, edge=edge):
+                same = (into[g, d, 129:130, :] == edge).astype(F32)
+                state[d, :, part] = into[g, d, 0:128, :] * same
 
             @pl.when(core != d)
-            def _(d=d, g=g, part=part):
+            def _(d=d, g=g, part=part, edge=edge):
                 top, end = join(other[g, d], into[g, d])
-                state[d, :, part] = top
-                if g == 0:
-                    state16[d] = end[:, 0:128]
-
-    def leave(d, k, prior):
-        docs = docs_ref[pl.ds(k, 1), :]
-        cum = reach[k, d]
-        carry = jnp.where(docs == prior, jnp.exp(cum), 0.0)
-        cols = jnp.concatenate([carry, cum, jnp.zeros((BLOCK - 2 * heads, BLOCK), F32)], axis=0).T
+                state[d, :, part] = top * (end[1:2] == edge).astype(F32)
+
+    def leave(d, k):
         before = state[d]
         given = jnp.dot(maps_ref[2 * d + 1, at(k), :], before.astype(BF16), preferred_element_type=F32)
-        if d == 0:
-            block, last = spread(cols[BLOCK - 8 :], heads, heads)[7:], docs[:, BLOCK - 1 :]
-        else:
-            block, last = spread(cols[:8], heads, heads)[:1], docs[:, :1]
-        state[d] = before * (jnp.exp(block) * (last == prior).astype(F32)) + local[d, k]
-        return given * spread(cols, 0, heads), last
-
-    def forward(k, prior):
-        part, last = leave(0, k, prior)
-        acc[at(k), :] += part
-        return last
-
-    lax.fori_loop(0, blocks, forward, state16[0, 1:2, 0:1])
-    squares[0] = jnp.zeros((BLOCK, 128), F32)
+        state[d] = before * gains[k, d : d + 1, :] + local[d, k]
+        return given * spread(columns[at(k), :], (4 + d) * heads, heads)
+
+    def forward(k, carry):
+        acc[at(k), :] += leave(0, k)
+        return carry
+
+    lax.fori_loop(0, blocks, forward, 0)
+    inverse[...] = jnp.zeros((BLOCK, 128), F32)
+    skip = jnp.concatenate([skip_ref[...], jnp.zeros((1, 128 - heads), F32)], axis=1)
+    skip = spread(jnp.broadcast_to(skip, (8, 128)), 0, heads)[:1]
     lane = iota((BLOCK, 128), 1)
 
-    def backward(step, prior):
+    def backward(step, carry):
         k = blocks - 1 - step
-        part, last = leave(1, k, prior)
+        part = leave(1, k)
         gate = gate_ref[at(k), :].astype(F32)
-        mixed = acc[at(k), :] + part + skip_ref[...] * x_ref[at(k), :].astype(F32)
+        mixed = acc[at(k), :] + part + skip * x_ref[at(k), :].astype(F32)
         gated = mixed * (gate / (1.0 + jnp.exp(-gate)))
         acc[at(k), :] = gated
-        squares[0] += jnp.where(lane == k, jnp.sum(gated * gated, axis=1, keepdims=True), 0.0)
-        return last
-
-    lax.fori_loop(0, blocks, backward, state16[1, 1:2, 0:1])
+        inverse[...] += jnp.where(lane == k, jnp.sum(gated * gated, axis=1, keepdims=True), 0.0)
+        return carry
+
+    lax.fori_loop(0, blocks, backward, 0)
+    kept = squares.shape[1]
+    squares[0] = inverse[...].T[0:kept]
     to_heads = [
         remote(squares.at[0], squares.at[o], send_h.at[o], recv_h.at[o], head_at(o))
         for o in range(1, head_ways)
@@ -268,7 +264,9 @@
     sum_all = squares[0]
     for o in range(1, head_ways):
         sum_all = sum_all + squares[o]
-    inverse[...] = lax.rsqrt(sum_all / (head_ways * width) + 1e-05)
+    rest = jnp.zeros((BLOCK - kept, 128), F32)
+    root = lax.rsqrt(sum_all / (head_ways * width) + 1e-05)
+    inverse[...] = jnp.concatenate([root, rest], axis=0).T
 
     def scale(k, carry):
         factor = jnp.sum(jnp.where(lane == k, inverse[...], 0.0), axis=1, keepdims=True)
@@ -287,8 +285,7 @@
     half = width // 2
     seq, head_ways = lax.axis_size("seq"), lax.axis_size("head")
     chips = seq // 2
-    docs = doc_ids.reshape(blocks, BLOCK).astype(F32)
-    skip = jnp.repeat(skip_weight, width // heads)[None, :]
+    docs = doc_ids.reshape(blocks, BLOCK)
     vmem = pl.BlockSpec(memory_space=pltpu.VMEM)
     return pl.pallas_call(
         functools.partial(kernel, (seq, head_ways, heads)),
@@ -304,11 +301,10 @@
             pltpu.VMEM((2, blocks, 128, width), F32),
             pltpu.VMEM((tokens, 128), F32),
             pltpu.VMEM((blocks, 2, heads, 128), F32),
-            pltpu.VMEM((blocks, 2, heads, 128), F32),
+            pltpu.VMEM((blocks, 2, width), F32),
             pltpu.VMEM((2, 128, width), F32),
-            pltpu.VMEM((2, 8, 128), F32),
             pltpu.VMEM((tokens, width), F32),
-            pltpu.VMEM((head_ways, BLOCK, 128), F32),
+            pltpu.VMEM((head_ways, -(-blocks // 8) * 8, 128), F32),
             pltpu.VMEM((BLOCK, 128), F32),
             pltpu.SemaphoreType.DMA,
             pltpu.SemaphoreType.DMA,
@@ -322,7 +318,7 @@
         compiler_params=pltpu.CompilerParams(
             collective_id=0, has_side_effects=True, vmem_limit_bytes=56 * 2**20
         ),
-    )(mixer_input, gate_input, state_maps, step_size, log_decay, skip, docs, norm_gain[None, :])
+    )(mixer_input, gate_input, state_maps, step_size, log_decay, skip_weight[None, :], docs, norm_gain[None, :])
 
 
 def solution(mesh):

time: 74.2 us -> 60.8 us (0.82)
  Pallas kernels: 67.4 us -> 56.7 us
  local copies, waits for them, and re-layouts: 5.26 us -> 3.86 us
  other arithmetic: 1.3 us -> 0 us
    pallas_call x1, Pallas kernels: 67.4 us -> 56.7 us  [local(): pl.pallas_call(functools.partial(kernel, (seq, head_ways, heads)), out_sh...]
    convert_element_type x1 -> x0, other arithmetic: 1.3 us -> none  [local(): docs = doc_ids.reshape(blocks, BLOCK).astype(F32)]
where the time goes in v2:
time: 60.8 us; the launch traced here: 60.6 us
  Pallas kernels  56.7 us (93%)
  local copies, waits for them, and re-layouts  3.86 us (6%)
    pallas_call x1, Pallas kernels, local(): pl.pallas_call(functools.partial(kernel, (seq, head_ways, heads)), out_sh...  56.7 us
    unnamed x1, local copies, waits for them, and re-layouts  3.86 us

profile of v2, /device:TPU:0, one launch (start us, length us, event | category | flops | bytes accessed | tf_op | source)
XLA Modules:
  0.0 60.6 jit_solution(1541261547885683566)
XLA Ops:
  0.0 56.7 %shard_map.82 = bf16[1536,1024]{1,0:T(8,128)(2,1)} custom-call(bf16[1536,1024]{1,0:T(8,128)(2,1)} %x_ref.1, bf16[1536,1024]{1,0:T(8,128)(2,1)} %gate_ref.1, bf16[4,1536,128]{2,1,0:T(8,128)(2,1)} %maps_ref.1, f32[2,16,1536]{2,1,0:T(8,128)} %step_ref.1, f32[2,16,1536]{2,1,0:T(8,128)} %decay_ref.1, f32[1,16]{1,0:T(1,128)} %bitcast.5, s32[12,128]{1,0:T(8,128)} %bitcast.3, ...), custom_call_target="tpu_custom_call" | custom-call | tf_op jit(solution)/shard_map/pallas_call | solution.py:290
  56.8 3.9 %copy.10 = bf16[1536,1024]{1,0:T(8,128)(2,1)} copy(bf16[1536,1024]{1,0:T(8,128)(2,1)} %shard_map.82) | data formatting | bytes 6291456

commit v3 on v2

--- a/solution.py
+++ b/solution.py
@@ -29,9 +29,9 @@
 
 
 def kernel(
-    sizes, x_ref, gate_ref, maps_ref, step_ref, decay_ref, skip_ref, docs_ref, gain_ref, out_ref,
-    own, other, total, slots, into, local, columns, rows, gains, state, acc, squares, inverse,
-    send_a, recv_a, send_b, recv_b, send_c, recv_c, send_h, recv_h,
+    sizes, x_ref, gate_hbm, maps_ref, step_ref, decay_ref, skip_ref, docs_ref, gain_ref, out_hbm,
+    own, other, total, slots, into, local, columns, rows, gains, state, acc, squares, inverse, gate_ref, silu, out_ref,
+    gate_sem, out_sems, send_a, recv_a, send_b, recv_b, send_c, recv_c, send_h, recv_h,
 ):
     seq, head_ways, heads = sizes
     chips = seq // 2
@@ -50,6 +50,8 @@
     def head_at(offset):
         return {"head": lax.rem(head_place + offset, head_ways)}
 
+    gate_copy = pltpu.make_async_copy(gate_hbm, gate_ref, gate_sem)
+    gate_copy.start()
     barrier = pltpu.get_barrier_semaphore()
     partners = [{"seq": sibling}]
     partners += [chip_at(o) for o in range(1, chips)] + [head_at(o) for o in range(1, head_ways)]
@@ -124,6 +126,10 @@
     low = iota((BLOCK, BLOCK), 1) < iota((BLOCK, BLOCK), 0)
     diagonal = iota((BLOCK, BLOCK), 1) == iota((BLOCK, BLOCK), 0)
     left = iota((BLOCK, BLOCK), 1) < 64
+    skip = jnp.concatenate([skip_ref[...], jnp.zeros((1, 128 - heads), F32)], axis=1)
+    skip = spread(jnp.broadcast_to(skip, (8, 128)), 0, heads)[:1]
+    lane = iota((BLOCK, 128), 1)
+    gate_copy.wait()
 
     def inside(k, carry):
         docs = jnp.broadcast_to(docs_ref[pl.ds(k, 1), :].astype(F32), (BLOCK, BLOCK))
@@ -147,9 +153,11 @@
                 weights.append((score * jnp.exp(power)).astype(BF16))
             none = jnp.zeros_like(x)
             values = jnp.concatenate([jnp.where(left, x, none), jnp.where(left, none, x)], axis=0)
-            acc[at(k), lanes] = jnp.dot(
+            acc[at(k), lanes] = skip[:, lanes] * x.astype(F32) + jnp.dot(
                 jnp.concatenate(weights, axis=1), values, preferred_element_type=F32
             )
+            gate = gate_ref[at(k), lanes].astype(F32)
+            silu[at(k), lanes] = gate / (1.0 + jnp.exp(-gate))
         return carry
 
     cut_a, cut_b = blocks // 4, blocks - blocks // 6
@@ -236,16 +244,11 @@
 
     lax.fori_loop(0, blocks, forward, 0)
     inverse[...] = jnp.zeros((BLOCK, 128), F32)
-    skip = jnp.concatenate([skip_ref[...], jnp.zeros((1, 128 - heads), F32)], axis=1)
-    skip = spread(jnp.broadcast_to(skip, (8, 128)), 0, heads)[:1]
-    lane = iota((BLOCK, 128), 1)
 
     def backward(step, carry):
         k = blocks - 1 - step
         part = leave(1, k)
-        gate = gate_ref[at(k), :].astype(F32)
-        mixed = acc[at(k), :] + part + skip * x_ref[at(k), :].astype(F32)
-        gated = mixed * (gate / (1.0 + jnp.exp(-gate)))
+        gated = (acc[at(k), :] + part) * silu[at(k), :]
         acc[at(k), :] = gated
         inverse[...] += jnp.where(lane == k, jnp.sum(gated * gated, axis=1, keepdims=True), 0.0)
         return carry
@@ -271,9 +274,15 @@
     def scale(k, carry):
         factor = jnp.sum(jnp.where(lane == k, inverse[...], 0.0), axis=1, keepdims=True)
         out_ref[at(k), :] = (acc[at(k), :] * factor * gain_ref[...]).astype(BF16)
+        pltpu.make_async_copy(out_ref.at[at(k)], out_hbm.at[at(k)], out_sems.at[k]).start()
+        return carry
+
+    def drain(k, carry):
+        pltpu.make_async_copy(out_ref.at[at(k)], out_hbm.at[at(k)], out_sems.at[k]).wait()
         return carry
 
     lax.fori_loop(0, blocks, scale, 0)
+    lax.fori_loop(0, blocks, drain, 0)
 
 
 def local(
@@ -287,11 +296,12 @@
     chips = seq // 2
     docs = doc_ids.reshape(blocks, BLOCK)
     vmem = pl.BlockSpec(memory_space=pltpu.VMEM)
+    hbm = pl.BlockSpec(memory_space=pl.ANY)
     return pl.pallas_call(
         functools.partial(kernel, (seq, head_ways, heads)),
         out_shape=jax.ShapeDtypeStruct((tokens, width), BF16),
-        in_specs=[vmem] * 8,
-        out_specs=vmem,
+        in_specs=[vmem, hbm] + [vmem] * 6,
+        out_specs=hbm,
         scratch_shapes=[
             pltpu.VMEM((2, 2, ROWS, half), F32),
             pltpu.VMEM((2, 2, ROWS, half), F32),
@@ -306,6 +316,11 @@
             pltpu.VMEM((tokens, width), F32),
             pltpu.VMEM((head_ways, -(-blocks // 8) * 8, 128), F32),
             pltpu.VMEM((BLOCK, 128), F32),
+            pltpu.VMEM((tokens, width), BF16),
+            pltpu.VMEM((tokens, width), F32),
+            pltpu.VMEM((tokens, width), BF16),
+            pltpu.SemaphoreType.DMA,
+            pltpu.SemaphoreType.DMA((blocks,)),
             pltpu.SemaphoreType.DMA,
             pltpu.SemaphoreType.DMA,
             pltpu.SemaphoreType.DMA((chips,)),

time: 60.8 us -> 57.8 us (0.951)
  Pallas kernels: 56.7 us -> 53.8 us
    pallas_call x1, Pallas kernels: 56.7 us -> 53.8 us  [local(): pl.pallas_call(functools.partial(kernel, (seq, head_ways, heads)), out_sh...]
where the time goes in v3:
time: 57.8 us; the launch traced here: 57.6 us
  Pallas kernels  53.8 us (93%)
  local copies, waits for them, and re-layouts  3.86 us (7%)
    pallas_call x1, Pallas kernels, local(): pl.pallas_call(functools.partial(kernel, (seq, head_ways, heads)), out_sh...  53.8 us
    unnamed x1, local copies, waits for them, and re-layouts  3.86 us

profile of v3, /device:TPU:0, one launch (start us, length us, event | category | flops | bytes accessed | tf_op | source)
XLA Modules:
  0.0 57.6 jit_solution(10507928452443095454)
XLA Ops:
  0.0 53.8 %shard_map.82 = bf16[1536,1024]{1,0:T(8,128)(2,1)} custom-call(bf16[1536,1024]{1,0:T(8,128)(2,1)} %x_ref.1, bf16[1536,1024]{1,0:T(8,128)(2,1)} %gate_hbm.1, bf16[4,1536,128]{2,1,0:T(8,128)(2,1)} %maps_ref.1, f32[2,16,1536]{2,1,0:T(8,128)} %step_ref.1, f32[2,16,1536]{2,1,0:T(8,128)} %decay_ref.1, f32[1,16]{1,0:T(1,128)} %bitcast.5, s32[12,128]{1,0:T(8,128)} %bitcast.3, ...), custom_call_target="tpu_custom_call" | custom-call | tf_op jit(solution)/shard_map/pallas_call | solution.py:300
  53.8 3.9 %copy.10 = bf16[1536,1024]{1,0:T(8,128)(2,1)} copy(bf16[1536,1024]{1,0:T(8,128)(2,1)} %shard_map.82) | data formatting | bytes 6291456
